TPU v7x, 32 devices: a whole 2x2x4 slice. The times are simulated.
32 devices in a mesh: grp: 2 (over x), seq: 16 (over z, y, core).
Axes of the slice: x: 2, y: 2, z: 4, core: 2. Of those that a mesh axis runs over, the one named last changes fastest.
Arguments:
- scalars: bfloat16 [256, 4096], P(None, ('grp', 'seq')), parts along dimension 1, may hold values from -6 to 6
- vectors: bfloat16 [3, 256, 4096], P(None, None, ('grp', 'seq')), parts along dimension 2, may hold values from -6 to 6
- w_qkw_s: bfloat16 [2, 768, 256], replicated, may hold values from -0.375 to 0.375
- w_qkw_v: bfloat16 [2, 768, 256], replicated, may hold values from -0.375 to 0.375
- w_out_s: bfloat16 [2, 256, 256], replicated, may hold values from -0.375 to 0.375
- w_out_v: bfloat16 [2, 256, 256], replicated, may hold values from -0.375 to 0.375
- w_up: bfloat16 [2, 1024, 256], replicated, may hold values from -0.375 to 0.375
- w_down: bfloat16 [2, 256, 1024], replicated, may hold values from -0.1875 to 0.1875
- w_mix: bfloat16 [2, 256, 256], replicated, may hold values from -0.375 to 0.375
- w_gate: bfloat16 [2, 256, 256], replicated, may hold values from -0.375 to 0.375
- gains: float32 [2, 4, 256], replicated, may hold values from 0.5 to 1.5
- pe_w1: float32 [2, 64, 16], replicated, may hold values from -24 to 24
- pe_w2: float32 [2, 64, 64], replicated, may hold values from -0.75 to 0.75
- pe_w3: float32 [2, 256, 64], replicated, may hold values from -1.5 to 1.5
- rates: float32 [2, 256], replicated, may hold values from 0.05 to 40
Outputs:
- scalars_out: bfloat16 [256, 4096], P(None, ('grp', 'seq')), parts along dimension 1
- vectors_out: bfloat16 [3, 256, 4096], P(None, None, ('grp', 'seq')), parts along dimension 2
There are 2 independent parts, one for each index of `grp`. A program takes and returns all parts, laid end to end along the dimension named above; an argument that names none is the same for every part. Nothing has to cross between parts.
All inputs are finite; a program needn't handle non-finite values.
Results may differ from a plain program's by a relative error of at most 0.02.
Values may be sent and summed in bfloat16 or wider, within the bound.
A program may use at most 64 MiB of HBM per device.

v0:
```python
import functools
import math

import jax
import jax.numpy as jnp
import numpy as np
from jax import lax
from jax.experimental import pallas as pl
from jax.experimental.pallas import tpu as pltpu
from jax.sharding import PartitionSpec as P


def filter_values(positions, length, first, second, third, decay):
    count = first.shape[1] // 2
    freqs = jnp.arange(1, count + 1, dtype=jnp.int32)
    turns = freqs[:, None] * positions[None, :] % length
    angle = turns.astype(jnp.float32) * (2.0 * math.pi / length)
    feats = jnp.concatenate([jnp.cos(angle), jnp.sin(angle)], axis=0)
    hid_one = jnp.sin(jnp.dot(first, feats, precision=lax.Precision.HIGHEST))
    hid_two = jnp.sin(jnp.dot(second, hid_one, precision=lax.Precision.HIGHEST))
    raw = jnp.dot(third, hid_two, precision=lax.Precision.HIGHEST)
    envelope = jnp.exp(-decay[:, None] * positions[None, :].astype(jnp.float32) / length)
    return (raw * envelope / math.sqrt(length)).astype(jnp.bfloat16)


def scalar_norm(field, gain):
    return field * lax.rsqrt(jnp.mean(field * field, axis=0, keepdims=True) + 1e-05) * gain[:, None]


def vector_norm(field, gain):
    return (
        field
        * lax.rsqrt(jnp.mean(field * field, axis=(0, 1), keepdims=True) + 1e-05)
        * gain[None, :, None]
    )


def square_table(count):
    index = jnp.arange(count, dtype=jnp.int32)
    turns = index[:, None] * index[None, :] % count
    angle = turns.astype(jnp.float32) * (2.0 * math.pi / count)
    return (jnp.cos(angle), jnp.sin(angle))


def make_tables(length):
    side_b = 1
    for candidate in range(1, math.isqrt(length) + 1):
        if length % candidate == 0:
            side_b = candidate
    side_a = length // side_b
    cos_b, sin_b = square_table(side_b)
    cos_a, sin_a = square_table(side_a)
    rows_b = jnp.arange(side_b, dtype=jnp.int32)
    cols_a = jnp.arange(side_a, dtype=jnp.int32)
    angle = (rows_b[:, None] * cols_a[None, :]).astype(jnp.float32) * (2.0 * math.pi / length)
    return (side_b, side_a, cos_b, sin_b, cos_a, sin_a, jnp.cos(angle), jnp.sin(angle))


def forward_dft(signal, tables):
    side_b, side_a, cos_b, sin_b, cos_a, sin_a, twist_r, twist_s = tables
    high = lax.Precision.HIGHEST
    first_r = jnp.einsum("cb,...ba->...ca", cos_b, signal, precision=high)
    first_i = -jnp.einsum("cb,...ba->...ca", sin_b, signal, precision=high)
    mid_r = first_r * twist_r + first_i * twist_s
    mid_i = first_i * twist_r - first_r * twist_s
    out_r = jnp.einsum("...ca,ad->...cd", mid_r, cos_a, precision=high) + jnp.einsum(
        "...ca,ad->...cd", mid_i, sin_a, precision=high
    )
    out_i = jnp.einsum("...ca,ad->...cd", mid_i, cos_a, precision=high) - jnp.einsum(
        "...ca,ad->...cd", mid_r, sin_a, precision=high
    )
    return (out_r, out_i)


def inverse_dft(spec_r, spec_i, tables):
    side_b, side_a, cos_b, sin_b, cos_a, sin_a, twist_r, twist_s = tables
    high = lax.Precision.HIGHEST
    back_r = jnp.einsum("...cd,da->...ca", spec_r, cos_a, precision=high) - jnp.einsum(
        "...cd,da->...ca", spec_i, sin_a, precision=high
    )
    back_i = jnp.einsum("...cd,da->...ca", spec_i, cos_a, precision=high) + jnp.einsum(
        "...cd,da->...ca", spec_r, sin_a, precision=high
    )
    turn_r = back_r * twist_r - back_i * twist_s
    turn_i = back_i * twist_r + back_r * twist_s
    whole = jnp.einsum("bc,...ca->...ba", cos_b, turn_r, precision=high) - jnp.einsum(
        "bc,...ca->...ba", sin_b, turn_i, precision=high
    )
    return whole / (side_b * side_a)


def convolve(fields, filt, tables):
    side_b, side_a = (tables[0], tables[1])
    length = side_b * side_a
    chans = fields.shape[1]
    stacked = jnp.concatenate([fields[0:1], filt[None], fields[1:]], axis=0).astype(jnp.float32)
    spec_r, spec_i = forward_dft(stacked.reshape(8, chans, side_b, side_a), tables)
    prod_r = spec_r[0] * spec_r[1] - spec_i[0] * spec_i[1]
    prod_i = spec_r[0] * spec_i[1] + spec_i[0] * spec_r[1]
    key_r, key_i = (spec_r[2:5], spec_i[2:5])
    val_r, val_i = (spec_r[5:8], spec_i[5:8])
    k_one_r, k_one_i = (jnp.roll(key_r, -1, axis=0), jnp.roll(key_i, -1, axis=0))
    k_two_r, k_two_i = (jnp.roll(key_r, -2, axis=0), jnp.roll(key_i, -2, axis=0))
    v_one_r, v_one_i = (jnp.roll(val_r, -1, axis=0), jnp.roll(val_i, -1, axis=0))
    v_two_r, v_two_i = (jnp.roll(val_r, -2, axis=0), jnp.roll(val_i, -2, axis=0))
    cross_r = k_one_r * v_two_r - k_one_i * v_two_i - (k_two_r * v_one_r - k_two_i * v_one_i)
    cross_i = k_one_r * v_two_i + k_one_i * v_two_r - (k_two_r * v_one_i + k_two_i * v_one_r)
    all_r = jnp.concatenate([prod_r[None], cross_r], axis=0)
    all_i = jnp.concatenate([prod_i[None], cross_i], axis=0)
    result = inverse_dft(all_r, all_i, tables).reshape(4, chans, length)
    inv_root = 1.0 / math.sqrt(length)
    scale = jnp.array([1.0, inv_root, inv_root, inv_root], dtype=jnp.float32)
    return (result * scale[:, None, None]).astype(jnp.bfloat16)


def plain_device(
    scalars,
    vectors,
    w_qkw_s,
    w_qkw_v,
    w_out_s,
    w_out_v,
    w_up,
    w_down,
    w_mix,
    w_gate,
    gains,
    pe_w1,
    pe_w2,
    pe_w3,
    rates,
):
    chans = scalars.shape[0]
    tok_local = scalars.shape[1]
    shards = lax.axis_size("seq")
    rank = lax.axis_index("seq")
    length = tok_local * shards
    depth = w_qkw_s.shape[0]
    tables = make_tables(length)
    local_pos = rank * tok_local + jnp.arange(tok_local, dtype=jnp.int32)
    made = jnp.stack(
        [
            filter_values(local_pos, length, pe_w1[layer], pe_w2[layer], pe_w3[layer], rates[layer])
            for layer in range(depth)
        ],
        axis=0,
    )
    filters = lax.all_to_all(made, "seq", split_axis=1, concat_axis=2, tiled=True)
    state_s = scalars.astype(jnp.float32)
    state_v = vectors.astype(jnp.float32)
    for layer in range(depth):
        normed_s = scalar_norm(state_s, gains[layer, 0]).astype(jnp.bfloat16)
        normed_v = vector_norm(state_v, gains[layer, 1]).astype(jnp.bfloat16)
        proj_s = jnp.dot(w_qkw_s[layer], normed_s, preferred_element_type=jnp.float32)
        query_s = proj_s[:chans].astype(jnp.bfloat16)
        signal_s = (proj_s[chans : 2 * chans] * proj_s[2 * chans :]).astype(jnp.bfloat16)
        proj_v = jnp.einsum(
            "oc,jct->jot", w_qkw_v[layer], normed_v, preferred_element_type=jnp.float32
        ).astype(jnp.bfloat16)
        query_v = proj_v[:, :chans]
        outgoing = jnp.concatenate(
            [signal_s[None], proj_v[:, chans : 2 * chans], proj_v[:, 2 * chans :]], axis=0
        )
        regrouped = lax.all_to_all(outgoing, "seq", split_axis=1, concat_axis=2, tiled=True)
        convolved = convolve(regrouped, filters[layer], tables)
        returned = lax.all_to_all(convolved, "seq", split_axis=2, concat_axis=1, tiled=True)
        conv_f = returned.astype(jnp.float32)
        qs_f = query_s.astype(jnp.float32)
        out_s = (
            qs_f * conv_f[0] + jnp.sum(query_v.astype(jnp.float32) * conv_f[1:], axis=0)
        ).astype(jnp.bfloat16)
        out_v = (qs_f[None] * conv_f[1:]).astype(jnp.bfloat16)
        state_s = state_s + jnp.dot(w_out_s[layer], out_s, preferred_element_type=jnp.float32)
        state_v = state_v + jnp.einsum(
            "oc,jct->jot", w_out_v[layer], out_v, preferred_element_type=jnp.float32
        )
        mlp_s = scalar_norm(state_s, gains[layer, 2]).astype(jnp.bfloat16)
        mlp_v = vector_norm(state_v, gains[layer, 3]).astype(jnp.bfloat16)
        hidden = jax.nn.gelu(
            jnp.dot(w_up[layer], mlp_s, preferred_element_type=jnp.float32)
        ).astype(jnp.bfloat16)
        gate = jax.nn.sigmoid(jnp.dot(w_gate[layer], mlp_s, preferred_element_type=jnp.float32))
        state_s = state_s + jnp.dot(w_down[layer], hidden, preferred_element_type=jnp.float32)
        state_v = (
            state_v
            + jnp.einsum("oc,jct->jot", w_mix[layer], mlp_v, preferred_element_type=jnp.float32)
            * gate[None]
        )
    return (state_s.astype(jnp.bfloat16), state_v.astype(jnp.bfloat16))


def reduced_sine(angle):
    turns = jnp.floor(angle * (1.0 / math.pi) + 0.5)
    rest = angle - turns * 3.140625
    rest = rest - turns * 9.67502593994140625e-4
    rest = rest - turns * 1.509957990978376432e-7
    half = turns * 0.5
    sign = 1.0 - 4.0 * (half - jnp.floor(half))
    sq = rest * rest
    poly = -2.5052108e-8
    poly = poly * sq + 2.7557319e-6
    poly = poly * sq - 1.9841270e-4
    poly = poly * sq + 8.3333333e-3
    poly = poly * sq - 1.6666667e-1
    return sign * (rest + rest * sq * poly)


def part_sum(one, two):
    if one is None:
        return two
    if two is None:
        return one
    return one + two


def part_diff(one, two):
    if two is None:
        return one
    if one is None:
        return -two
    return one - two


def turn(value, step, count):
    step = step % count
    real, imag = value
    if step == 0:
        return value
    if 4 * step == count:
        return (None if imag is None else -imag, real)
    if 4 * step == 3 * count:
        return (imag, None if real is None else -real)
    cos, sin = (math.cos(2 * math.pi * step / count), math.sin(2 * math.pi * step / count))
    if imag is None:
        return (real * cos, real * sin)
    if real is None:
        return (imag * -sin, imag * cos)
    return (real * cos - imag * sin, imag * cos + real * sin)


def real_fft(fields):
    count = len(fields)
    if count == 1:
        return [(fields[0], None)]
    if count == 2:
        return [(fields[0] + fields[1], None), (fields[0] - fields[1], None)]
    even, odd = (real_fft(fields[0::2]), real_fft(fields[1::2]))
    out = [None] * (count // 2 + 1)
    for k in range(count // 4 + 1):
        spun = turn(odd[k], -k, count)
        out[k] = (part_sum(even[k][0], spun[0]), part_sum(even[k][1], spun[1]))
        back = (part_diff(even[k][0], spun[0]), part_diff(spun[1], even[k][1]))
        if count // 2 - k != k:
            out[count // 2 - k] = back
    return out


def inverse_real_fft(spec, count):
    if count == 1:
        return [spec[0][0]]
    if count == 2:
        return [spec[0][0] + spec[1][0], spec[0][0] - spec[1][0]]
    even, odd = ([], [])
    for k in range(count // 4 + 1):
        one, two = (spec[k], spec[count // 2 - k])
        if 4 * k == count:
            even.append((one[0] * 2.0, None))
            odd.append((one[1] * -2.0, None))
            continue
        even.append((part_sum(one[0], two[0]), part_diff(one[1], two[1])))
        diff = (part_diff(one[0], two[0]), part_sum(one[1], two[1]))
        odd.append(turn(diff, k, count))
    out = [None] * count
    out[0::2] = inverse_real_fft(even, count // 2)
    out[1::2] = inverse_real_fft(odd, count // 2)
    return out


def local_tables(shards, tok_local):
    length = shards * tok_local
    freq = np.arange(shards // 2 + 1)[:, None, None] + shards * np.arange(tok_local)[None, None, :]
    angle = (np.arange(tok_local)[None, :, None] * freq % length) * (2.0 * np.pi / length)
    cos, sin = (np.cos(angle), np.sin(angle))
    fore = np.concatenate(
        [np.concatenate([cos, -sin], axis=2), np.concatenate([sin, cos], axis=2)], axis=1
    )
    cos, sin = (cos.transpose(0, 2, 1), sin.transpose(0, 2, 1))
    back = np.concatenate(
        [np.concatenate([cos, sin], axis=2), np.concatenate([-sin, cos], axis=2)], axis=1
    )
    return (jnp.asarray(fore, jnp.bfloat16), jnp.asarray(back / length, jnp.bfloat16))


def layers_kernel(
    shards,
    scalars,
    vectors,
    w_qkw_s,
    w_qkw_v,
    w_out_s,
    w_out_v,
    w_up,
    w_down,
    w_mix,
    w_gate,
    gains,
    pe_w1,
    pe_w2,
    pe_w3,
    rates,
    fore,
    back,
    scalars_out,
    vectors_out,
    state_s,
    state_v,
    query_s,
    query_v,
    sent_f,
    got_f,
    sent_x,
    got_x,
    sent_y,
    got_y,
    mid,
    inv,
    send_sem,
    recv_sem,
):
    grp = lax.axis_index("grp")
    me = lax.axis_index("seq")
    chans, tok = scalars.shape
    own = chans // shards
    length = shards * tok
    depth = w_qkw_s.shape[0]
    half = shards // 2 + 1
    f32, bf16 = (jnp.float32, jnp.bfloat16)
    mesh_id = pl.DeviceIdType.MESH

    barrier = pltpu.get_barrier_semaphore()

    def greet(step, carry):
        peer = lax.rem(me + step, shards)
        pl.semaphore_signal(barrier, inc=1, device_id=(grp, peer), device_id_type=mesh_id)
        return carry

    lax.fori_loop(1, shards, greet, 0)

    def copy_of(kind, src, dst, peer, lane):
        return pltpu.make_async_remote_copy(
            src_ref=src,
            dst_ref=dst,
            send_sem=send_sem.at[kind, peer],
            recv_sem=recv_sem.at[kind, lane],
            device_id=(grp, peer),
            device_id_type=mesh_id,
        )

    def send(kind, src, dst, rows):
        def body(step, carry):
            peer = lax.rem(me + step, shards)
            copy_of(kind, src.at[peer, rows], dst.at[me, rows], peer, me).start()
            return carry

        lax.fori_loop(1, shards, body, 0)
        dst[pl.ds(me, 1), rows] = src[pl.ds(me, 1), rows]

    def receive(kind, dst, rows):
        def body(step, carry):
            peer = lax.rem(me + step, shards)
            copy_of(kind, dst.at[peer, rows], dst.at[peer, rows], peer, peer).wait_recv()
            return carry

        lax.fori_loop(1, shards, body, 0)

    def sent(kind, src, rows):
        def body(step, carry):
            peer = lax.rem(me + step, shards)
            copy_of(kind, src.at[peer, rows], src.at[peer, rows], peer, peer).wait_send()
            return carry

        lax.fori_loop(1, shards, body, 0)

    def column(row):
        return jnp.broadcast_to(row, (tok, chans)).T

    def normed_scalar(field, gain):
        return (
            field * lax.rsqrt(jnp.mean(field * field, axis=0, keepdims=True) + 1e-05) * gain
        ).astype(bf16)

    def normed_vector(fields, gain):
        total = sum(jnp.sum(field * field, axis=0, keepdims=True) for field in fields)
        scale = lax.rsqrt(total * (1.0 / (3 * chans)) + 1e-05)
        return jnp.concatenate([(field * scale * gain).astype(bf16) for field in fields], axis=1)

    def make_filter(layer):
        count = pe_w1.shape[2] // 2
        row = lax.broadcasted_iota(jnp.int32, (2 * count, tok), 0)
        pos = me * tok + lax.broadcasted_iota(jnp.int32, (2 * count, tok), 1)
        is_cos = row < count
        turns = (jnp.where(is_cos, row + 1, row + 1 - count) * pos).astype(f32)
        turns = turns + jnp.where(is_cos, length / 4.0, 0.0)
        turns = turns - length * jnp.floor(turns * (1.0 / length))
        feats = reduced_sine(turns * (2.0 * math.pi / length))
        high = lax.Precision.HIGHEST
        one = reduced_sine(jnp.dot(pe_w1[layer], feats, precision=high, preferred_element_type=f32))
        two = reduced_sine(jnp.dot(pe_w2[layer], one, precision=high, preferred_element_type=f32))
        raw = jnp.dot(pe_w3[layer], two, precision=high, preferred_element_type=f32)
        place = (me * tok + lax.broadcasted_iota(jnp.int32, (chans, tok), 1)).astype(f32)
        rate = column(rates[pl.ds(layer, 1), :])
        made = raw * jnp.exp(-rate * place * (1.0 / length)) * (1.0 / math.sqrt(length))
        sent_f[:, layer * own : (layer + 1) * own, :] = made.astype(bf16).reshape(shards, own, tok)

    def spread(fields, row):
        spec = real_fft(fields)
        for k in range(half):
            real, imag = spec[k]
            mid[k, row : row + own, 0:tok] = real.astype(bf16)
            if imag is None:
                imag = jnp.zeros_like(real)
            mid[k, row : row + own, tok : 2 * tok] = imag.astype(bf16)

    def gather_back(layer, signal, scale):
        spec = []
        for k in range(half):
            imag = None if k in (0, half - 1) else inv[k, signal * own : (signal + 1) * own, tok : 2 * tok]
            spec.append((inv[k, signal * own : (signal + 1) * own, 0:tok], imag))
        out = inverse_real_fft(spec, shards)
        for r in range(shards):
            value = out[r] if scale is None else out[r] * scale
            sent_y[layer, r, signal * own : (signal + 1) * own, :] = value.astype(bf16)

    def incoming(ref, row):
        return [ref[r, row : row + own, :].astype(f32) for r in range(shards)]

    def times(one, two):
        return (one[0] * two[0] - one[1] * two[1], one[0] * two[1] + one[1] * two[0])

    state_s[...] = scalars[...].astype(f32)
    state_v[...] = vectors[...].astype(f32)
    vec_rows, sca_rows = (pl.ds(0, 6 * own), pl.ds(6 * own, own))
    for layer in range(depth):
        base = 4 * layer
        fields = [state_v[j] for j in range(3)]
        vn = normed_vector(fields, column(gains[layer, 1:2, :]))
        pv = jnp.dot(w_qkw_v[layer, chans:, :], vn, preferred_element_type=f32).astype(bf16)
        for j in range(3):
            cols = slice(j * tok, (j + 1) * tok)
            sent_x[layer, :, j * own : (j + 1) * own, :] = pv[:chans, cols].reshape(shards, own, tok)
            sent_x[layer, :, (3 + j) * own : (4 + j) * own, :] = pv[chans:, cols].reshape(
                shards, own, tok
            )
        if layer == 0:
            pl.semaphore_wait(barrier, shards - 1)
        send(base, sent_x.at[layer], got_x.at[layer], vec_rows)
        sn = normed_scalar(state_s[...], column(gains[layer, 0:1, :]))
        ps = jnp.dot(w_qkw_s[layer, chans:, :], sn, preferred_element_type=f32)
        sent_x[layer, :, 6 * own : 7 * own, :] = (
            (ps[:chans] * ps[chans:]).astype(bf16).reshape(shards, own, tok)
        )
        send(base + 1, sent_x.at[layer], got_x.at[layer], sca_rows)
        if layer == 0:
            for each in range(depth):
                make_filter(each)
            send(4 * depth, sent_f, got_f, pl.ds(0, depth * own))
        query_s[...] = jnp.dot(w_qkw_s[layer, :chans, :], sn, preferred_element_type=f32).astype(bf16)
        query_v[...] = jnp.dot(w_qkw_v[layer, :chans, :], vn, preferred_element_type=f32).astype(bf16)

        receive(base, got_x.at[layer], vec_rows)
        for signal in range(6):
            spread(incoming(got_x.at[layer], signal * own), signal * own)
        for k in range(half):
            spec = jnp.dot(mid[k, : 6 * own, :], fore[k], preferred_element_type=f32)
            parts = [
                (spec[i * own : (i + 1) * own, :tok], spec[i * own : (i + 1) * own, tok:])
                for i in range(6)
            ]
            rows = []
            for j in range(3):
                plus = times(parts[(j + 1) % 3], parts[3 + (j + 2) % 3])
                minus = times(parts[(j + 2) % 3], parts[3 + (j + 1) % 3])
                rows.append(jnp.concatenate([plus[0] - minus[0], plus[1] - minus[1]], axis=1))
            inv[k, : 3 * own, :] = jnp.dot(
                jnp.concatenate(rows, axis=0).astype(bf16), back[k], preferred_element_type=f32
            )
        for signal in range(3):
            gather_back(layer, signal, 1.0 / math.sqrt(length))
        send(base + 2, sent_y.at[layer], got_y.at[layer], pl.ds(0, 3 * own))

        receive(base + 1, got_x.at[layer], sca_rows)
        if layer == 0:
            receive(4 * depth, got_f, pl.ds(0, depth * own))
        spread(incoming(got_x.at[layer], 6 * own), 6 * own)
        spread(incoming(got_f, layer * own), 7 * own)
        for k in range(half):
            spec = jnp.dot(mid[k, 6 * own :, :], fore[k], preferred_element_type=f32)
            prod = times((spec[:own, :tok], spec[:own, tok:]), (spec[own:, :tok], spec[own:, tok:]))
            inv[k, 3 * own :, :] = jnp.dot(
                jnp.concatenate(prod, axis=1).astype(bf16), back[k], preferred_element_type=f32
            )
        gather_back(layer, 3, None)
        send(base + 3, sent_y.at[layer], got_y.at[layer], pl.ds(3 * own, own))

        receive(base + 2, got_y.at[layer], pl.ds(0, 3 * own))
        qs = query_s[...].astype(f32)
        out_v = []
        mixed = None
        for j in range(3):
            field = got_y[layer, :, j * own : (j + 1) * own, :].reshape(chans, tok).astype(f32)
            term = query_v[:, j * tok : (j + 1) * tok].astype(f32) * field
            mixed = term if mixed is None else mixed + term
            out_v.append((qs * field).astype(bf16))
        moved = jnp.dot(w_out_v[layer], jnp.concatenate(out_v, axis=1), preferred_element_type=f32)
        fields = [state_v[j] + moved[:, j * tok : (j + 1) * tok] for j in range(3)]
        vm = normed_vector(fields, column(gains[layer, 3:4, :]))
        mix = jnp.dot(w_mix[layer], vm, preferred_element_type=f32)
        receive(base + 3, got_y.at[layer], pl.ds(3 * own, own))
        field = got_y[layer, :, 3 * own : 4 * own, :].reshape(chans, tok).astype(f32)
        out_s = (qs * field + mixed).astype(bf16)
        now_s = state_s[...] + jnp.dot(w_out_s[layer], out_s, preferred_element_type=f32)
        sm = normed_scalar(now_s, column(gains[layer, 2:3, :]))
        hidden = jax.nn.gelu(jnp.dot(w_up[layer], sm, preferred_element_type=f32)).astype(bf16)
        gate = jax.nn.sigmoid(jnp.dot(w_gate[layer], sm, preferred_element_type=f32))
        now_s = now_s + jnp.dot(w_down[layer], hidden, preferred_element_type=f32)
        now_v = [fields[j] + mix[:, j * tok : (j + 1) * tok] * gate for j in range(3)]
        if layer + 1 < depth:
            state_s[...] = now_s
            for j in range(3):
                state_v[j] = now_v[j]
        else:
            scalars_out[...] = now_s.astype(bf16)
            for j in range(3):
                vectors_out[j] = now_v[j].astype(bf16)
    for layer in range(depth):
        base = 4 * layer
        sent(base, sent_x.at[layer], vec_rows)
        sent(base + 1, sent_x.at[layer], sca_rows)
        sent(base + 2, sent_y.at[layer], pl.ds(0, 3 * own))
        sent(base + 3, sent_y.at[layer], pl.ds(3 * own, own))
    sent(4 * depth, sent_f, pl.ds(0, depth * own))


def per_device(*arrays):
    scalars, vectors, w_qkw_s = arrays[:3]
    chans, tok = scalars.shape
    shards = lax.axis_size("seq")
    depth = w_qkw_s.shape[0]
    own = chans // shards
    if tok % 128 or own % 16 or chans % shards or shards & (shards - 1) or shards < 4:
        return plain_device(*arrays)
    half = shards // 2 + 1
    fore, back = local_tables(shards, tok)
    f32, bf16 = (jnp.float32, jnp.bfloat16)
    whole = pl.BlockSpec(memory_space=pltpu.VMEM)
    return pl.pallas_call(
        functools.partial(layers_kernel, shards),
        out_shape=(
            jax.ShapeDtypeStruct(scalars.shape, bf16),
            jax.ShapeDtypeStruct(vectors.shape, bf16),
        ),
        in_specs=[whole] * (len(arrays) + 2),
        out_specs=(whole, whole),
        scratch_shapes=[
            pltpu.VMEM((chans, tok), f32),
            pltpu.VMEM((3, chans, tok), f32),
            pltpu.VMEM((chans, tok), bf16),
            pltpu.VMEM((chans, 3 * tok), bf16),
            pltpu.VMEM((shards, depth * own, tok), bf16),
            pltpu.VMEM((shards, depth * own, tok), bf16),
            pltpu.VMEM((depth, shards, 7 * own, tok), bf16),
            pltpu.VMEM((depth, shards, 7 * own, tok), bf16),
            pltpu.VMEM((depth, shards, 4 * own, tok), bf16),
            pltpu.VMEM((depth, shards, 4 * own, tok), bf16),
            pltpu.VMEM((half, 8 * own, 2 * tok), bf16),
            pltpu.VMEM((half, 4 * own, 2 * tok), f32),
            pltpu.SemaphoreType.DMA((4 * depth + 1, shards)),
            pltpu.SemaphoreType.DMA((4 * depth + 1, shards)),
        ],
        compiler_params=pltpu.CompilerParams(
            collective_id=0, has_side_effects=True, vmem_limit_bytes=40 * 1024 * 1024
        ),
        name="hyena_layers",
    )(*arrays, fore, back)


def solution(mesh):
    in_specs = (
        P(None, ("grp", "seq")),
        P(None, None, ("grp", "seq")),
        P(),
        P(),
        P(),
        P(),
        P(),
        P(),
        P(),
        P(),
        P(),
        P(),
        P(),
        P(),
        P(),
    )
    out_specs = (P(None, ("grp", "seq")), P(None, None, ("grp", "seq")))
    return jax.shard_map(
        per_device, mesh=mesh, in_specs=in_specs, out_specs=out_specs, check_vma=False
    )
```

profile of v0, /device:TPU:0, one launch (start us, length us, event | category | flops | bytes accessed | tf_op | source)
XLA Modules:
  0.0 72.4 jit_solution(12153963922265391745)
XLA Ops:
  0.6 0.8 %copy.19.pe_w1 = f32[2,64,16]{2,1,0:T(8,128)S(1)} copy(f32[2,64,16]{1,2,0:T(8,128)} %param.28) | data formatting | bytes 16384 | tf_op args[11]
  1.4 1.0 %copy.20.pe_w3 = f32[2,256,64]{2,1,0:T(8,128)S(1)} copy(f32[2,256,64]{1,2,0:T(8,128)} %param.30) | data formatting | bytes 262144 | tf_op args[13]
  2.5 0.0 copy-start
  2.5 1.3 %copy-done = bf16[9,256,256]{2,1,0:T(8,128)(2,1)S(1)} copy-done((bf16[9,256,256]{2,1,0:T(8,128)(2,1)S(1)}, bf16[9,256,256]{2,1,0:T(8,128)(2,1)}, u32[]{:S(2)}) %copy-start) | copy-done | bytes 1179672
  3.7 0.0 copy-start.1
  3.7 1.3 %copy-done.1 = bf16[9,256,256]{2,1,0:T(8,128)(2,1)S(1)} copy-done((bf16[9,256,256]{2,1,0:T(8,128)(2,1)S(1)}, bf16[9,256,256]{2,1,0:T(8,128)(2,1)}, u32[]{:S(2)}) %copy-start.1) | copy-done | bytes 1179672
  5.0 0.0 copy-start.2
  5.0 1.2 %copy-done.2 = bf16[2,1024,256]{2,1,0:T(8,128)(2,1)S(1)} copy-done((bf16[2,1024,256]{2,1,0:T(8,128)(2,1)S(1)}, bf16[2,1024,256]{2,1,0:T(8,128)(2,1)}, u32[]{:S(2)}) %copy-start.2) | copy-done | bytes 1048600
  6.2 0.0 copy-start.3
  6.2 1.2 %copy-done.3 = bf16[2,256,1024]{2,1,0:T(8,128)(2,1)S(1)} copy-done((bf16[2,256,1024]{2,1,0:T(8,128)(2,1)S(1)}, bf16[2,256,1024]{2,1,0:T(8,128)(2,1)}, u32[]{:S(2)}) %copy-start.3) | copy-done | bytes 1048600
  7.5 0.0 copy-start.4
  7.5 1.1 %copy-done.4 = bf16[2,768,256]{2,1,0:T(8,128)(2,1)S(1)} copy-done((bf16[2,768,256]{2,1,0:T(8,128)(2,1)S(1)}, bf16[2,768,256]{2,1,0:T(8,128)(2,1)}, u32[]{:S(2)}) %copy-start.4) | copy-done | bytes 786456
  8.6 0.0 copy-start.5
  8.6 1.1 %copy-done.5 = bf16[2,768,256]{2,1,0:T(8,128)(2,1)S(1)} copy-done((bf16[2,768,256]{2,1,0:T(8,128)(2,1)S(1)}, bf16[2,768,256]{2,1,0:T(8,128)(2,1)}, u32[]{:S(2)}) %copy-start.5) | copy-done | bytes 786456
  9.7 0.0 copy-start.6
  9.7 0.9 %copy-done.6 = bf16[2,256,256]{2,1,0:T(8,128)(2,1)S(1)} copy-done((bf16[2,256,256]{2,1,0:T(8,128)(2,1)S(1)}, bf16[2,256,256]{2,1,0:T(8,128)(2,1)}, u32[]{:S(2)}) %copy-start.6) | copy-done | bytes 262168
  10.7 0.0 copy-start.7
  10.7 0.9 %copy-done.7 = bf16[2,256,256]{2,1,0:T(8,128)(2,1)S(1)} copy-done((bf16[2,256,256]{2,1,0:T(8,128)(2,1)S(1)}, bf16[2,256,256]{2,1,0:T(8,128)(2,1)}, u32[]{:S(2)}) %copy-start.7) | copy-done | bytes 262168
  11.6 0.0 copy-start.8
  11.6 0.9 %copy-done.8 = bf16[2,256,256]{2,1,0:T(8,128)(2,1)S(1)} copy-done((bf16[2,256,256]{2,1,0:T(8,128)(2,1)S(1)}, bf16[2,256,256]{2,1,0:T(8,128)(2,1)}, u32[]{:S(2)}) %copy-start.8) | copy-done | bytes 262168
  12.6 0.0 copy-start.9
  12.6 0.9 %copy-done.9 = bf16[2,256,256]{2,1,0:T(8,128)(2,1)S(1)} copy-done((bf16[2,256,256]{2,1,0:T(8,128)(2,1)S(1)}, bf16[2,256,256]{2,1,0:T(8,128)(2,1)}, u32[]{:S(2)}) %copy-start.9) | copy-done | bytes 262168
  13.5 0.0 copy-start.10
  13.5 0.9 %copy-done.10 = bf16[3,256,128]{2,1,0:T(8,128)(2,1)S(1)} copy-done((bf16[3,256,128]{2,1,0:T(8,128)(2,1)S(1)}, bf16[3,256,128]{2,1,0:T(8,128)(2,1)}, u32[]{:S(2)}) %copy-start.10) | copy-done | bytes 196632
  14.5 0.0 copy-start.11
  14.5 0.8 %copy-done.11 = bf16[256,128]{1,0:T(8,128)(2,1)S(1)} copy-done((bf16[256,128]{1,0:T(8,128)(2,1)S(1)}, bf16[256,128]{1,0:T(8,128)(2,1)}, u32[]{:S(2)}) %copy-start.11) | copy-done | bytes 65560
  15.3 0.0 copy-start.12
  15.3 0.8 %copy-done.12 = f32[2,64,64]{2,1,0:T(8,128)S(1)} copy-done((f32[2,64,64]{2,1,0:T(8,128)S(1)}, f32[2,64,64]{2,1,0:T(8,128)}, u32[]{:S(2)}) %copy-start.12) | copy-done | bytes 32792
  16.1 0.0 copy-start.13
  16.1 0.7 copy-done.13
  16.8 0.0 copy-start.14
  16.8 0.7 copy-done.14
  17.5 53.6 %hyena_layers.1 = (bf16[256,128]{1,0:T(8,128)(2,1)S(1)}, bf16[3,256,128]{2,1,0:T(8,128)(2,1)S(1)}) custom-call(bf16[256,128]{1,0:T(8,128)(2,1)S(1)} %copy-done.11, bf16[3,256,128]{2,1,0:T(8,128)(2,1)S(1)} %copy-done.10, bf16[2,768,256]{2,1,0:T(8,128)(2,1)S(1)} %copy-done.4, bf16[2,768,256]{2,1,0:T(8,128)(2,1)S(1)} %copy-done.5, ...), custom_call_target="tpu_custom_call" | custom-call | tf_op jit(solution)/shard_map/hyena_layers/pallas_call | solution.py:556
  71.1 0.6 copy.23
  71.8 0.7 copy.24
Async XLA Ops:
  2.5 1.3 %copy-start = (bf16[9,256,256]{2,1,0:T(8,128)(2,1)S(1)}, bf16[9,256,256]{2,1,0:T(8,128)(2,1)}, u32[]{:S(2)}) copy-start(bf16[9,256,256]{2,1,0:T(8,128)(2,1)} %constant.5.clone.back) | copy-start | bytes 3538948
  3.7 1.3 %copy-start.1 = (bf16[9,256,256]{2,1,0:T(8,128)(2,1)S(1)}, bf16[9,256,256]{2,1,0:T(8,128)(2,1)}, u32[]{:S(2)}) copy-start(bf16[9,256,256]{2,1,0:T(8,128)(2,1)} %constant.4.clone.fore) | copy-start | bytes 3538948
  5.0 1.2 %copy-start.2 = (bf16[2,1024,256]{2,1,0:T(8,128)(2,1)S(1)}, bf16[2,1024,256]{2,1,0:T(8,128)(2,1)}, u32[]{:S(2)}) copy-start(bf16[2,1024,256]{2,1,0:T(8,128)(2,1)} %w_up.1) | copy-start | bytes 3145732
  6.2 1.2 %copy-start.3 = (bf16[2,256,1024]{2,1,0:T(8,128)(2,1)S(1)}, bf16[2,256,1024]{2,1,0:T(8,128)(2,1)}, u32[]{:S(2)}) copy-start(bf16[2,256,1024]{2,1,0:T(8,128)(2,1)} %w_down.1) | copy-start | bytes 3145732
  7.5 1.1 %copy-start.4 = (bf16[2,768,256]{2,1,0:T(8,128)(2,1)S(1)}, bf16[2,768,256]{2,1,0:T(8,128)(2,1)}, u32[]{:S(2)}) copy-start(bf16[2,768,256]{2,1,0:T(8,128)(2,1)} %w_qkw_s.1) | copy-start | bytes 2359300
  8.6 1.1 %copy-start.5 = (bf16[2,768,256]{2,1,0:T(8,128)(2,1)S(1)}, bf16[2,768,256]{2,1,0:T(8,128)(2,1)}, u32[]{:S(2)}) copy-start(bf16[2,768,256]{2,1,0:T(8,128)(2,1)} %w_qkw_v.1) | copy-start | bytes 2359300
  9.7 0.9 %copy-start.6 = (bf16[2,256,256]{2,1,0:T(8,128)(2,1)S(1)}, bf16[2,256,256]{2,1,0:T(8,128)(2,1)}, u32[]{:S(2)}) copy-start(bf16[2,256,256]{2,1,0:T(8,128)(2,1)} %w_out_s.1) | copy-start | bytes 786436
  10.7 0.9 %copy-start.7 = (bf16[2,256,256]{2,1,0:T(8,128)(2,1)S(1)}, bf16[2,256,256]{2,1,0:T(8,128)(2,1)}, u32[]{:S(2)}) copy-start(bf16[2,256,256]{2,1,0:T(8,128)(2,1)} %w_out_v.1) | copy-start | bytes 786436
  11.6 0.9 %copy-start.8 = (bf16[2,256,256]{2,1,0:T(8,128)(2,1)S(1)}, bf16[2,256,256]{2,1,0:T(8,128)(2,1)}, u32[]{:S(2)}) copy-start(bf16[2,256,256]{2,1,0:T(8,128)(2,1)} %w_mix.1) | copy-start | bytes 786436
  12.6 0.9 %copy-start.9 = (bf16[2,256,256]{2,1,0:T(8,128)(2,1)S(1)}, bf16[2,256,256]{2,1,0:T(8,128)(2,1)}, u32[]{:S(2)}) copy-start(bf16[2,256,256]{2,1,0:T(8,128)(2,1)} %w_gate.1) | copy-start | bytes 786436
  13.5 0.9 %copy-start.10 = (bf16[3,256,128]{2,1,0:T(8,128)(2,1)S(1)}, bf16[3,256,128]{2,1,0:T(8,128)(2,1)}, u32[]{:S(2)}) copy-start(bf16[3,256,128]{2,1,0:T(8,128)(2,1)} %vectors.1) | copy-start | bytes 589828
  14.5 0.8 %copy-start.11 = (bf16[256,128]{1,0:T(8,128)(2,1)S(1)}, bf16[256,128]{1,0:T(8,128)(2,1)}, u32[]{:S(2)}) copy-start(bf16[256,128]{1,0:T(8,128)(2,1)} %scalars.1) | copy-start | bytes 196612
  15.3 0.8 %copy-start.12 = (f32[2,64,64]{2,1,0:T(8,128)S(1)}, f32[2,64,64]{2,1,0:T(8,128)}, u32[]{:S(2)}) copy-start(f32[2,64,64]{2,1,0:T(8,128)} %pe_w2.1) | copy-start | bytes 98308
  16.1 0.7 copy-start.13
  16.8 0.7 copy-start.14
where the time goes:
time: 73.2 us; the launch traced here: 72.4 us
  Pallas kernels  53.6 us (73%)
  local copies, waits for them, and re-layouts  18.2 us (25%)
    pallas_call x1, Pallas kernels, per_device(): pl.pallas_call(functools.partial(layers_kernel, shards), out_shape=(jax.S...  53.6 us
    unnamed x34, local copies, waits for them, and re-layouts  18.2 us

commit v1 on v0

--- a/solution.py
+++ b/solution.py
@@ -284,49 +284,27 @@
     fore = np.concatenate(
         [np.concatenate([cos, -sin], axis=2), np.concatenate([sin, cos], axis=2)], axis=1
     )
-    cos, sin = (cos.transpose(0, 2, 1), sin.transpose(0, 2, 1))
-    back = np.concatenate(
-        [np.concatenate([cos, sin], axis=2), np.concatenate([-sin, cos], axis=2)], axis=1
-    )
-    return (jnp.asarray(fore, jnp.bfloat16), jnp.asarray(back / length, jnp.bfloat16))
-
-
-def layers_kernel(
-    shards,
-    scalars,
-    vectors,
-    w_qkw_s,
-    w_qkw_v,
-    w_out_s,
-    w_out_v,
-    w_up,
-    w_down,
-    w_mix,
-    w_gate,
-    gains,
-    pe_w1,
-    pe_w2,
-    pe_w3,
-    rates,
-    fore,
-    back,
-    scalars_out,
-    vectors_out,
-    state_s,
-    state_v,
-    query_s,
-    query_v,
-    sent_f,
-    got_f,
-    sent_x,
-    got_x,
-    sent_y,
-    got_y,
-    mid,
-    inv,
-    send_sem,
-    recv_sem,
-):
+    return jnp.asarray(fore, jnp.float32)
+
+
+def layers_kernel(shards, count, *refs):
+    outside, refs = (refs[:count], refs[count:])
+    scalars_out, vectors_out, *refs = refs
+    inside, refs = (refs[:count], refs[count:])
+    load_sem, state_s, state_v, query_s, query_v, *refs = refs
+    fore, made_f, sent_x, got_x, sent_y, got_y, mid, inv, send_sem, recv_sem = refs
+    scalars, vectors, w_qkw_s, w_qkw_v, w_out_s, w_out_v, w_up, w_down, w_mix, w_gate = inside[:10]
+    gains, pe_w1, pe_w2, pe_w3, rates, fore_wide = inside[10:]
+    loads = [
+        pltpu.make_async_copy(outside[i], inside[i], load_sem.at[i]) for i in range(count)
+    ]
+    for i in (1, 3, 10, 0, 2, 11, 12, 13, 14, 15, 5, 8, 4, 6, 9, 7):
+        loads[i].start()
+
+    def need(*places):
+        for i in places:
+            loads[i].wait()
+
     grp = lax.axis_index("grp")
     me = lax.axis_index("seq")
     chans, tok = scalars.shape
@@ -357,12 +335,14 @@
         )
 
     def send(kind, src, dst, rows):
-        def body(step, carry):
+        def body(turn, carry):
+            side = lax.rem(turn, 2)
+            step = shards // 2 + (1 - 2 * side) * ((turn + 1) // 2)
             peer = lax.rem(me + step, shards)
             copy_of(kind, src.at[peer, rows], dst.at[me, rows], peer, me).start()
             return carry
 
-        lax.fori_loop(1, shards, body, 0)
+        lax.fori_loop(0, shards - 1, body, 0)
         dst[pl.ds(me, 1), rows] = src[pl.ds(me, 1), rows]
 
     def receive(kind, dst, rows):
@@ -395,22 +375,39 @@
         return jnp.concatenate([(field * scale * gain).astype(bf16) for field in fields], axis=1)
 
     def make_filter(layer):
-        count = pe_w1.shape[2] // 2
-        row = lax.broadcasted_iota(jnp.int32, (2 * count, tok), 0)
-        pos = me * tok + lax.broadcasted_iota(jnp.int32, (2 * count, tok), 1)
-        is_cos = row < count
-        turns = (jnp.where(is_cos, row + 1, row + 1 - count) * pos).astype(f32)
-        turns = turns + jnp.where(is_cos, length / 4.0, 0.0)
-        turns = turns - length * jnp.floor(turns * (1.0 / length))
-        feats = reduced_sine(turns * (2.0 * math.pi / length))
+        freqs = pe_w1.shape[1] // 2
         high = lax.Precision.HIGHEST
-        one = reduced_sine(jnp.dot(pe_w1[layer], feats, precision=high, preferred_element_type=f32))
-        two = reduced_sine(jnp.dot(pe_w2[layer], one, precision=high, preferred_element_type=f32))
-        raw = jnp.dot(pe_w3[layer], two, precision=high, preferred_element_type=f32)
-        place = (me * tok + lax.broadcasted_iota(jnp.int32, (chans, tok), 1)).astype(f32)
-        rate = column(rates[pl.ds(layer, 1), :])
-        made = raw * jnp.exp(-rate * place * (1.0 / length)) * (1.0 / math.sqrt(length))
-        sent_f[:, layer * own : (layer + 1) * own, :] = made.astype(bf16).reshape(shards, own, tok)
+        lhs_rows = (((0,), (0,)), ((), ()))
+        pick = (
+            lax.broadcasted_iota(jnp.int32, (own, chans), 1)
+            == me * own + lax.broadcasted_iota(jnp.int32, (own, chans), 0)
+        ).astype(f32)
+        rate = jnp.sum(pick * rates[layer : layer + 1, :], axis=1, keepdims=True)
+        third = lax.dot_general(
+            pick, pe_w3[layer], (((1,), (1,)), ((), ())), precision=high, preferred_element_type=f32
+        )
+        span = tok * math.gcd(4, shards)
+        for start in range(0, length, span):
+            row = lax.broadcasted_iota(jnp.int32, (2 * freqs, span), 0)
+            pos = start + lax.broadcasted_iota(jnp.int32, (2 * freqs, span), 1)
+            is_cos = row < freqs
+            turns = (jnp.where(is_cos, row + 1, row + 1 - freqs) * pos).astype(f32)
+            turns = turns + jnp.where(is_cos, length / 4.0, 0.0)
+            turns = turns - length * jnp.floor(turns * (1.0 / length))
+            feats = reduced_sine(turns * (2.0 * math.pi / length))
+            one = reduced_sine(
+                lax.dot_general(
+                    pe_w1[layer], feats, lhs_rows, precision=high, preferred_element_type=f32
+                )
+            )
+            two = reduced_sine(
+                jnp.dot(pe_w2[layer], one, precision=high, preferred_element_type=f32)
+            )
+            raw = jnp.dot(third, two, precision=high, preferred_element_type=f32)
+            place = (start + lax.broadcasted_iota(jnp.int32, (own, span), 1)).astype(f32)
+            made = raw * jnp.exp(-rate * place * (1.0 / length)) * (1.0 / math.sqrt(length))
+            for r in range(span // tok):
+                made_f[start // tok + r] = made[:, r * tok : (r + 1) * tok].astype(bf16)
 
     def spread(fields, row):
         spec = real_fft(fields)
@@ -428,8 +425,7 @@
             spec.append((inv[k, signal * own : (signal + 1) * own, 0:tok], imag))
         out = inverse_real_fft(spec, shards)
         for r in range(shards):
-            value = out[r] if scale is None else out[r] * scale
-            sent_y[layer, r, signal * own : (signal + 1) * own, :] = value.astype(bf16)
+            sent_y[layer, r, signal * own : (signal + 1) * own, :] = (out[r] * scale).astype(bf16)
 
     def incoming(ref, row):
         return [ref[r, row : row + own, :].astype(f32) for r in range(shards)]
@@ -437,12 +433,19 @@
     def times(one, two):
         return (one[0] * two[0] - one[1] * two[1], one[0] * two[1] + one[1] * two[0])
 
-    state_s[...] = scalars[...].astype(f32)
+    def undo(spec, k):
+        return lax.dot_general(
+            spec, fore[k], (((1,), (1,)), ((), ())), preferred_element_type=f32
+        )
+
+    need(1)
     state_v[...] = vectors[...].astype(f32)
     vec_rows, sca_rows = (pl.ds(0, 6 * own), pl.ds(6 * own, own))
     for layer in range(depth):
         base = 4 * layer
         fields = [state_v[j] for j in range(3)]
+        if layer == 0:
+            need(10, 3)
         vn = normed_vector(fields, column(gains[layer, 1:2, :]))
         pv = jnp.dot(w_qkw_v[layer, chans:, :], vn, preferred_element_type=f32).astype(bf16)
         for j in range(3):
@@ -454,18 +457,24 @@
         if layer == 0:
             pl.semaphore_wait(barrier, shards - 1)
         send(base, sent_x.at[layer], got_x.at[layer], vec_rows)
+        if layer == 0:
+            need(0, 2)
+            state_s[...] = scalars[...].astype(f32)
         sn = normed_scalar(state_s[...], column(gains[layer, 0:1, :]))
         ps = jnp.dot(w_qkw_s[layer, chans:, :], sn, preferred_element_type=f32)
         sent_x[layer, :, 6 * own : 7 * own, :] = (
             (ps[:chans] * ps[chans:]).astype(bf16).reshape(shards, own, tok)
         )
         send(base + 1, sent_x.at[layer], got_x.at[layer], sca_rows)
-        if layer == 0:
-            for each in range(depth):
-                make_filter(each)
-            send(4 * depth, sent_f, got_f, pl.ds(0, depth * own))
         query_s[...] = jnp.dot(w_qkw_s[layer, :chans, :], sn, preferred_element_type=f32).astype(bf16)
         query_v[...] = jnp.dot(w_qkw_v[layer, :chans, :], vn, preferred_element_type=f32).astype(bf16)
+        if layer == 0:
+            need(11, 12, 13, 14)
+        make_filter(layer)
+        spread(incoming(made_f, 0), 7 * own)
+        if layer == 0:
+            need(15)
+            fore[...] = fore_wide[...].astype(bf16)
 
         receive(base, got_x.at[layer], vec_rows)
         for signal in range(6):
@@ -481,27 +490,22 @@
                 plus = times(parts[(j + 1) % 3], parts[3 + (j + 2) % 3])
                 minus = times(parts[(j + 2) % 3], parts[3 + (j + 1) % 3])
                 rows.append(jnp.concatenate([plus[0] - minus[0], plus[1] - minus[1]], axis=1))
-            inv[k, : 3 * own, :] = jnp.dot(
-                jnp.concatenate(rows, axis=0).astype(bf16), back[k], preferred_element_type=f32
-            )
+            inv[k, : 3 * own, :] = undo(jnp.concatenate(rows, axis=0).astype(bf16), k)
         for signal in range(3):
-            gather_back(layer, signal, 1.0 / math.sqrt(length))
+            gather_back(layer, signal, 1.0 / (length * math.sqrt(length)))
         send(base + 2, sent_y.at[layer], got_y.at[layer], pl.ds(0, 3 * own))
 
         receive(base + 1, got_x.at[layer], sca_rows)
-        if layer == 0:
-            receive(4 * depth, got_f, pl.ds(0, depth * own))
         spread(incoming(got_x.at[layer], 6 * own), 6 * own)
-        spread(incoming(got_f, layer * own), 7 * own)
         for k in range(half):
             spec = jnp.dot(mid[k, 6 * own :, :], fore[k], preferred_element_type=f32)
             prod = times((spec[:own, :tok], spec[:own, tok:]), (spec[own:, :tok], spec[own:, tok:]))
-            inv[k, 3 * own :, :] = jnp.dot(
-                jnp.concatenate(prod, axis=1).astype(bf16), back[k], preferred_element_type=f32
-            )
-        gather_back(layer, 3, None)
+            inv[k, 3 * own :, :] = undo(jnp.concatenate(prod, axis=1).astype(bf16), k)
+        gather_back(layer, 3, 1.0 / length)
         send(base + 3, sent_y.at[layer], got_y.at[layer], pl.ds(3 * own, own))
 
+        if layer == 0:
+            need(5, 8, 4, 6, 9, 7)
         receive(base + 2, got_y.at[layer], pl.ds(0, 3 * own))
         qs = query_s[...].astype(f32)
         out_v = []
@@ -538,7 +542,6 @@
         sent(base + 1, sent_x.at[layer], sca_rows)
         sent(base + 2, sent_y.at[layer], pl.ds(0, 3 * own))
         sent(base + 3, sent_y.at[layer], pl.ds(3 * own, own))
-    sent(4 * depth, sent_f, pl.ds(0, depth * own))
 
 
 def per_device(*arrays):
@@ -550,38 +553,44 @@
     if tok % 128 or own % 16 or chans % shards or shards & (shards - 1) or shards < 4:
         return plain_device(*arrays)
     half = shards // 2 + 1
-    fore, back = local_tables(shards, tok)
     f32, bf16 = (jnp.float32, jnp.bfloat16)
+    arrays = list(arrays)
+    arrays[11] = jnp.swapaxes(arrays[11], 1, 2)
+    arrays[13] = jnp.swapaxes(arrays[13], 1, 2)
+    arrays.append(local_tables(shards, tok))
+    count = len(arrays)
     whole = pl.BlockSpec(memory_space=pltpu.VMEM)
     return pl.pallas_call(
-        functools.partial(layers_kernel, shards),
+        functools.partial(layers_kernel, shards, count),
         out_shape=(
             jax.ShapeDtypeStruct(scalars.shape, bf16),
             jax.ShapeDtypeStruct(vectors.shape, bf16),
         ),
-        in_specs=[whole] * (len(arrays) + 2),
+        in_specs=[pl.BlockSpec(memory_space=pltpu.HBM)] * count,
         out_specs=(whole, whole),
-        scratch_shapes=[
+        scratch_shapes=[pltpu.VMEM(array.shape, array.dtype) for array in arrays]
+        + [
+            pltpu.SemaphoreType.DMA((count,)),
             pltpu.VMEM((chans, tok), f32),
             pltpu.VMEM((3, chans, tok), f32),
             pltpu.VMEM((chans, tok), bf16),
             pltpu.VMEM((chans, 3 * tok), bf16),
-            pltpu.VMEM((shards, depth * own, tok), bf16),
-            pltpu.VMEM((shards, depth * own, tok), bf16),
+            pltpu.VMEM((half, 2 * tok, 2 * tok), bf16),
+            pltpu.VMEM((shards, own, tok), bf16),
             pltpu.VMEM((depth, shards, 7 * own, tok), bf16),
             pltpu.VMEM((depth, shards, 7 * own, tok), bf16),
             pltpu.VMEM((depth, shards, 4 * own, tok), bf16),
             pltpu.VMEM((depth, shards, 4 * own, tok), bf16),
             pltpu.VMEM((half, 8 * own, 2 * tok), bf16),
             pltpu.VMEM((half, 4 * own, 2 * tok), f32),
-            pltpu.SemaphoreType.DMA((4 * depth + 1, shards)),
-            pltpu.SemaphoreType.DMA((4 * depth + 1, shards)),
+            pltpu.SemaphoreType.DMA((4 * depth, shards)),
+            pltpu.SemaphoreType.DMA((4 * depth, shards)),
         ],
         compiler_params=pltpu.CompilerParams(
-            collective_id=0, has_side_effects=True, vmem_limit_bytes=40 * 1024 * 1024
+            collective_id=0, has_side_effects=True, vmem_limit_bytes=63 * 1024 * 1024
         ),
         name="hyena_layers",
-    )(*arrays, fore, back)
+    )(*arrays)
 
 
 def solution(mesh):

time: 73.2 us -> 54.9 us (0.75)
  local copies, waits for them, and re-layouts: 18.2 us -> 3.09 us
  Pallas kernels: 53.6 us -> 50.9 us
    unnamed x34 -> x2, local copies, waits for them, and re-layouts: 18.2 us -> 3.09 us
    pallas_call x1, Pallas kernels: 53.6 us -> 50.9 us  [per_device(): pl.pallas_call(functools.partial(layers_kernel, shards, count), out_shape...]
where the time goes in v1:
time: 54.9 us; the launch traced here: 54.7 us
  Pallas kernels  50.9 us (93%)
  local copies, waits for them, and re-layouts  3.09 us (6%)
  between operations  0.64 us (1%)
    pallas_call x1, Pallas kernels, per_device(): pl.pallas_call(functools.partial(layers_kernel, shards, count), out_shape...  50.9 us
    unnamed x2, local copies, waits for them, and re-layouts  3.09 us

profile of v1, /device:TPU:0, one launch (start us, length us, event | category | flops | bytes accessed | tf_op | source)
XLA Modules:
  0.0 54.7 jit_solution(4011899985758649419)
XLA Ops:
  0.6 50.9 %hyena_layers.1 = (bf16[256,128]{1,0:T(8,128)(2,1)}, bf16[3,256,128]{2,1,0:T(8,128)(2,1)}) custom-call(bf16[256,128]{1,0:T(8,128)(2,1)} %refs_0_.1, bf16[3,256,128]{2,1,0:T(8,128)(2,1)} %refs_1_.1, bf16[2,768,256]{2,1,0:T(8,128)(2,1)} %refs_2_.1, bf16[2,768,256]{2,1,0:T(8,128)(2,1)} %refs_3_.1, bf16[2,256,256]{2,1,0:T(8,128)(2,1)} %refs_4_.1, ...), custom_call_target="tpu_custom_call" | custom-call | tf_op jit(solution)/shard_map/hyena_layers/pallas_call | solution.py:563
  51.6 1.5 %copy.20 = bf16[256,128]{1,0:T(8,128)(2,1)} copy(bf16[256,128]{1,0:T(8,128)(2,1)} %get-tuple-element.4) | data formatting | bytes 131072
  53.1 1.6 %copy.21 = bf16[3,256,128]{2,1,0:T(8,128)(2,1)} copy(bf16[3,256,128]{2,1,0:T(8,128)(2,1)} %get-tuple-element.5) | data formatting | bytes 393216

commit v2 on v1

--- a/solution.py
+++ b/solution.py
@@ -292,7 +292,7 @@
     scalars_out, vectors_out, *refs = refs
     inside, refs = (refs[:count], refs[count:])
     load_sem, state_s, state_v, query_s, query_v, *refs = refs
-    fore, made_f, sent_x, got_x, sent_y, got_y, mid, inv, send_sem, recv_sem = refs
+    fore, made_f, sent_x, got_x, sent_y, got_y, mid, spec, inv, send_sem, recv_sem = refs
     scalars, vectors, w_qkw_s, w_qkw_v, w_out_s, w_out_v, w_up, w_down, w_mix, w_gate = inside[:10]
     gains, pe_w1, pe_w2, pe_w3, rates, fore_wide = inside[10:]
     loads = [
@@ -324,12 +324,12 @@
 
     lax.fori_loop(1, shards, greet, 0)
 
-    def copy_of(kind, src, dst, peer, lane):
+    def copy_of(kind, src, dst, peer):
         return pltpu.make_async_remote_copy(
             src_ref=src,
             dst_ref=dst,
-            send_sem=send_sem.at[kind, peer],
-            recv_sem=recv_sem.at[kind, lane],
+            send_sem=send_sem.at[kind],
+            recv_sem=recv_sem.at[kind],
             device_id=(grp, peer),
             device_id_type=mesh_id,
         )
@@ -339,27 +339,21 @@
             side = lax.rem(turn, 2)
             step = shards // 2 + (1 - 2 * side) * ((turn + 1) // 2)
             peer = lax.rem(me + step, shards)
-            copy_of(kind, src.at[peer, rows], dst.at[me, rows], peer, me).start()
+            copy_of(kind, src.at[peer, rows], dst.at[me, rows], peer).start()
             return carry
 
         lax.fori_loop(0, shards - 1, body, 0)
         dst[pl.ds(me, 1), rows] = src[pl.ds(me, 1), rows]
 
+    def all_of(kind, ref, rows):
+        blocks = ref.at[pl.ds(0, shards - 1), rows]
+        return copy_of(kind, blocks, blocks, lax.rem(me + 1, shards))
+
     def receive(kind, dst, rows):
-        def body(step, carry):
-            peer = lax.rem(me + step, shards)
-            copy_of(kind, dst.at[peer, rows], dst.at[peer, rows], peer, peer).wait_recv()
-            return carry
-
-        lax.fori_loop(1, shards, body, 0)
+        all_of(kind, dst, rows).wait_recv()
 
     def sent(kind, src, rows):
-        def body(step, carry):
-            peer = lax.rem(me + step, shards)
-            copy_of(kind, src.at[peer, rows], src.at[peer, rows], peer, peer).wait_send()
-            return carry
-
-        lax.fori_loop(1, shards, body, 0)
+        all_of(kind, src, rows).wait_send()
 
     def column(row):
         return jnp.broadcast_to(row, (tok, chans)).T
@@ -440,23 +434,52 @@
 
     need(1)
     state_v[...] = vectors[...].astype(f32)
-    vec_rows, sca_rows = (pl.ds(0, 6 * own), pl.ds(6 * own, own))
+    x_rows = (pl.ds(0, 4 * own), pl.ds(4 * own, 2 * own), pl.ds(6 * own, own))
+    y_rows = (pl.ds(0, own), pl.ds(own, 2 * own), pl.ds(3 * own, own))
+    key_slot, val_slot = ((4, 0, 1), (5, 2, 3))
+
+    def part(k, slot):
+        return (
+            spec[k, slot * own : (slot + 1) * own, :tok],
+            spec[k, slot * own : (slot + 1) * own, tok:],
+        )
+
+    def cross(k, j):
+        one, two = ((j + 1) % 3, (j + 2) % 3)
+        plus = times(part(k, key_slot[one]), part(k, val_slot[two]))
+        minus = times(part(k, key_slot[two]), part(k, val_slot[one]))
+        return jnp.concatenate([plus[0] - minus[0], plus[1] - minus[1]], axis=1)
+
+    def transform(first, last):
+        for k in range(half):
+            spec[k, first * own : last * own, :] = jnp.dot(
+                mid[k, first * own : last * own, :], fore[k], preferred_element_type=f32
+            )
+
     for layer in range(depth):
-        base = 4 * layer
+        base = 6 * layer
         fields = [state_v[j] for j in range(3)]
         if layer == 0:
             need(10, 3)
         vn = normed_vector(fields, column(gains[layer, 1:2, :]))
-        pv = jnp.dot(w_qkw_v[layer, chans:, :], vn, preferred_element_type=f32).astype(bf16)
-        for j in range(3):
-            cols = slice(j * tok, (j + 1) * tok)
-            sent_x[layer, :, j * own : (j + 1) * own, :] = pv[:chans, cols].reshape(shards, own, tok)
-            sent_x[layer, :, (3 + j) * own : (4 + j) * own, :] = pv[chans:, cols].reshape(
+        w_kw = w_qkw_v[layer, chans:, :]
+        pv = jnp.dot(w_kw, vn[:, tok:], preferred_element_type=f32).astype(bf16)
+        for slot in range(4):
+            rows = slice((slot // 2) * chans, (slot // 2 + 1) * chans)
+            cols = slice((slot % 2) * tok, (slot % 2 + 1) * tok)
+            sent_x[layer, :, slot * own : (slot + 1) * own, :] = pv[rows, cols].reshape(
                 shards, own, tok
             )
         if layer == 0:
             pl.semaphore_wait(barrier, shards - 1)
-        send(base, sent_x.at[layer], got_x.at[layer], vec_rows)
+        send(base, sent_x.at[layer], got_x.at[layer], x_rows[0])
+        pv = jnp.dot(w_kw, vn[:, :tok], preferred_element_type=f32).astype(bf16)
+        for slot in range(2):
+            rows = slice(slot * chans, (slot + 1) * chans)
+            sent_x[layer, :, (4 + slot) * own : (5 + slot) * own, :] = pv[rows].reshape(
+                shards, own, tok
+            )
+        send(base + 1, sent_x.at[layer], got_x.at[layer], x_rows[1])
         if layer == 0:
             need(0, 2)
             state_s[...] = scalars[...].astype(f32)
@@ -465,7 +488,7 @@
         sent_x[layer, :, 6 * own : 7 * own, :] = (
             (ps[:chans] * ps[chans:]).astype(bf16).reshape(shards, own, tok)
         )
-        send(base + 1, sent_x.at[layer], got_x.at[layer], sca_rows)
+        send(base + 2, sent_x.at[layer], got_x.at[layer], x_rows[2])
         query_s[...] = jnp.dot(w_qkw_s[layer, :chans, :], sn, preferred_element_type=f32).astype(bf16)
         query_v[...] = jnp.dot(w_qkw_v[layer, :chans, :], vn, preferred_element_type=f32).astype(bf16)
         if layer == 0:
@@ -476,41 +499,43 @@
             need(15)
             fore[...] = fore_wide[...].astype(bf16)
 
-        receive(base, got_x.at[layer], vec_rows)
-        for signal in range(6):
-            spread(incoming(got_x.at[layer], signal * own), signal * own)
+        receive(base, got_x.at[layer], x_rows[0])
+        for slot in range(4):
+            spread(incoming(got_x.at[layer], slot * own), slot * own)
+        transform(0, 4)
         for k in range(half):
-            spec = jnp.dot(mid[k, : 6 * own, :], fore[k], preferred_element_type=f32)
-            parts = [
-                (spec[i * own : (i + 1) * own, :tok], spec[i * own : (i + 1) * own, tok:])
-                for i in range(6)
-            ]
-            rows = []
-            for j in range(3):
-                plus = times(parts[(j + 1) % 3], parts[3 + (j + 2) % 3])
-                minus = times(parts[(j + 2) % 3], parts[3 + (j + 1) % 3])
-                rows.append(jnp.concatenate([plus[0] - minus[0], plus[1] - minus[1]], axis=1))
-            inv[k, : 3 * own, :] = undo(jnp.concatenate(rows, axis=0).astype(bf16), k)
-        for signal in range(3):
+            inv[k, :own, :] = undo(cross(k, 0).astype(bf16), k)
+        gather_back(layer, 0, 1.0 / (length * math.sqrt(length)))
+        send(base + 3, sent_y.at[layer], got_y.at[layer], y_rows[0])
+
+        receive(base + 1, got_x.at[layer], x_rows[1])
+        for slot in range(4, 6):
+            spread(incoming(got_x.at[layer], slot * own), slot * own)
+        transform(4, 6)
+        for k in range(half):
+            both = jnp.concatenate([cross(k, 1), cross(k, 2)], axis=0)
+            inv[k, own : 3 * own, :] = undo(both.astype(bf16), k)
+        for signal in range(1, 3):
             gather_back(layer, signal, 1.0 / (length * math.sqrt(length)))
-        send(base + 2, sent_y.at[layer], got_y.at[layer], pl.ds(0, 3 * own))
-
-        receive(base + 1, got_x.at[layer], sca_rows)
+        send(base + 4, sent_y.at[layer], got_y.at[layer], y_rows[1])
+
+        receive(base + 2, got_x.at[layer], x_rows[2])
         spread(incoming(got_x.at[layer], 6 * own), 6 * own)
+        transform(6, 8)
         for k in range(half):
-            spec = jnp.dot(mid[k, 6 * own :, :], fore[k], preferred_element_type=f32)
-            prod = times((spec[:own, :tok], spec[:own, tok:]), (spec[own:, :tok], spec[own:, tok:]))
+            prod = times(part(k, 6), part(k, 7))
             inv[k, 3 * own :, :] = undo(jnp.concatenate(prod, axis=1).astype(bf16), k)
         gather_back(layer, 3, 1.0 / length)
-        send(base + 3, sent_y.at[layer], got_y.at[layer], pl.ds(3 * own, own))
+        send(base + 5, sent_y.at[layer], got_y.at[layer], y_rows[2])
 
         if layer == 0:
             need(5, 8, 4, 6, 9, 7)
-        receive(base + 2, got_y.at[layer], pl.ds(0, 3 * own))
         qs = query_s[...].astype(f32)
         out_v = []
         mixed = None
         for j in range(3):
+            if j < 2:
+                receive(base + 3 + j, got_y.at[layer], y_rows[j])
             field = got_y[layer, :, j * own : (j + 1) * own, :].reshape(chans, tok).astype(f32)
             term = query_v[:, j * tok : (j + 1) * tok].astype(f32) * field
             mixed = term if mixed is None else mixed + term
@@ -519,7 +544,7 @@
         fields = [state_v[j] + moved[:, j * tok : (j + 1) * tok] for j in range(3)]
         vm = normed_vector(fields, column(gains[layer, 3:4, :]))
         mix = jnp.dot(w_mix[layer], vm, preferred_element_type=f32)
-        receive(base + 3, got_y.at[layer], pl.ds(3 * own, own))
+        receive(base + 5, got_y.at[layer], y_rows[2])
         field = got_y[layer, :, 3 * own : 4 * own, :].reshape(chans, tok).astype(f32)
         out_s = (qs * field + mixed).astype(bf16)
         now_s = state_s[...] + jnp.dot(w_out_s[layer], out_s, preferred_element_type=f32)
@@ -537,11 +562,9 @@
             for j in range(3):
                 vectors_out[j] = now_v[j].astype(bf16)
     for layer in range(depth):
-        base = 4 * layer
-        sent(base, sent_x.at[layer], vec_rows)
-        sent(base + 1, sent_x.at[layer], sca_rows)
-        sent(base + 2, sent_y.at[layer], pl.ds(0, 3 * own))
-        sent(base + 3, sent_y.at[layer], pl.ds(3 * own, own))
+        for i in range(3):
+            sent(6 * layer + i, sent_x.at[layer], x_rows[i])
+            sent(6 * layer + 3 + i, sent_y.at[layer], y_rows[i])
 
 
 def per_device(*arrays):
@@ -582,9 +605,10 @@
             pltpu.VMEM((depth, shards, 4 * own, tok), bf16),
             pltpu.VMEM((depth, shards, 4 * own, tok), bf16),
             pltpu.VMEM((half, 8 * own, 2 * tok), bf16),
+            pltpu.VMEM((half, 8 * own, 2 * tok), f32),
             pltpu.VMEM((half, 4 * own, 2 * tok), f32),
-            pltpu.SemaphoreType.DMA((4 * depth, shards)),
-            pltpu.SemaphoreType.DMA((4 * depth, shards)),
+            pltpu.SemaphoreType.DMA((6 * depth,)),
+            pltpu.SemaphoreType.DMA((6 * depth,)),
         ],
         compiler_params=pltpu.CompilerParams(
             collective_id=0, has_side_effects=True, vmem_limit_bytes=63 * 1024 * 1024

time: 54.9 us -> 51.4 us (0.936)
  Pallas kernels: 50.9 us -> 47.5 us
    pallas_call x1, Pallas kernels: 50.9 us -> 47.5 us  [per_device(): pl.pallas_call(functools.partial(layers_kernel, shards, count), out_shape...]
where the time goes in v2:
time: 51.4 us; the launch traced here: 51.2 us
  Pallas kernels  47.5 us (92%)
  local copies, waits for them, and re-layouts  3.09 us (6%)
  between operations  0.64 us (1%)
    pallas_call x1, Pallas kernels, per_device(): pl.pallas_call(functools.partial(layers_kernel, shards, count), out_shape...  47.5 us
    unnamed x2, local copies, waits for them, and re-layouts  3.09 us

profile of v2, /device:TPU:0, one launch (start us, length us, event | category | flops | bytes accessed | tf_op | source)
XLA Modules:
  0.0 51.2 jit_solution(8048256522884295386)
XLA Ops:
  0.6 47.5 %hyena_layers.1 = (bf16[256,128]{1,0:T(8,128)(2,1)}, bf16[3,256,128]{2,1,0:T(8,128)(2,1)}) custom-call(bf16[256,128]{1,0:T(8,128)(2,1)} %refs_0_.1, bf16[3,256,128]{2,1,0:T(8,128)(2,1)} %refs_1_.1, bf16[2,768,256]{2,1,0:T(8,128)(2,1)} %refs_2_.1, bf16[2,768,256]{2,1,0:T(8,128)(2,1)} %refs_3_.1, bf16[2,256,256]{2,1,0:T(8,128)(2,1)} %refs_4_.1, ...), custom_call_target="tpu_custom_call" | custom-call | tf_op jit(solution)/shard_map/hyena_layers/pallas_call | solution.py:586
  48.1 1.5 %copy.20 = bf16[256,128]{1,0:T(8,128)(2,1)} copy(bf16[256,128]{1,0:T(8,128)(2,1)} %get-tuple-element.4) | data formatting | bytes 131072
  49.6 1.6 %copy.21 = bf16[3,256,128]{2,1,0:T(8,128)(2,1)} copy(bf16[3,256,128]{2,1,0:T(8,128)(2,1)} %get-tuple-element.5) | data formatting | bytes 393216

commit v3 on v2

--- a/solution.py
+++ b/solution.py
@@ -291,7 +291,7 @@
     outside, refs = (refs[:count], refs[count:])
     scalars_out, vectors_out, *refs = refs
     inside, refs = (refs[:count], refs[count:])
-    load_sem, state_s, state_v, query_s, query_v, *refs = refs
+    load_sem, state_s, state_v, columns, ready_s, query_s, query_v, *refs = refs
     fore, made_f, sent_x, got_x, sent_y, got_y, mid, spec, inv, send_sem, recv_sem = refs
     scalars, vectors, w_qkw_s, w_qkw_v, w_out_s, w_out_v, w_up, w_down, w_mix, w_gate = inside[:10]
     gains, pe_w1, pe_w2, pe_w3, rates, fore_wide = inside[10:]
@@ -456,12 +456,18 @@
                 mid[k, first * own : last * own, :], fore[k], preferred_element_type=f32
             )
 
+    def finish_scalar(layer):
+        wide = jnp.dot(w_up[layer], ready_s[...], preferred_element_type=f32)
+        hidden = jax.nn.gelu(wide).astype(bf16)
+        return state_s[...] + jnp.dot(w_down[layer], hidden, preferred_element_type=f32)
+
     for layer in range(depth):
         base = 6 * layer
         fields = [state_v[j] for j in range(3)]
         if layer == 0:
             need(10, 3)
-        vn = normed_vector(fields, column(gains[layer, 1:2, :]))
+            columns[1] = column(gains[0, 1:2, :])
+        vn = normed_vector(fields, columns[4 * layer + 1])
         w_kw = w_qkw_v[layer, chans:, :]
         pv = jnp.dot(w_kw, vn[:, tok:], preferred_element_type=f32).astype(bf16)
         for slot in range(4):
@@ -483,7 +489,10 @@
         if layer == 0:
             need(0, 2)
             state_s[...] = scalars[...].astype(f32)
-        sn = normed_scalar(state_s[...], column(gains[layer, 0:1, :]))
+            columns[0] = column(gains[0, 0:1, :])
+        else:
+            state_s[...] = finish_scalar(layer - 1)
+        sn = normed_scalar(state_s[...], columns[4 * layer])
         ps = jnp.dot(w_qkw_s[layer, chans:, :], sn, preferred_element_type=f32)
         sent_x[layer, :, 6 * own : 7 * own, :] = (
             (ps[:chans] * ps[chans:]).astype(bf16).reshape(shards, own, tok)
@@ -492,6 +501,8 @@
         query_s[...] = jnp.dot(w_qkw_s[layer, :chans, :], sn, preferred_element_type=f32).astype(bf16)
         query_v[...] = jnp.dot(w_qkw_v[layer, :chans, :], vn, preferred_element_type=f32).astype(bf16)
         if layer == 0:
+            for place in range(2, 4 * depth):
+                columns[place] = column(gains[place // 4, place % 4 : place % 4 + 1, :])
             need(11, 12, 13, 14)
         make_filter(layer)
         spread(incoming(made_f, 0), 7 * own)
@@ -542,29 +553,39 @@
             out_v.append((qs * field).astype(bf16))
         moved = jnp.dot(w_out_v[layer], jnp.concatenate(out_v, axis=1), preferred_element_type=f32)
         fields = [state_v[j] + moved[:, j * tok : (j + 1) * tok] for j in range(3)]
-        vm = normed_vector(fields, column(gains[layer, 3:4, :]))
+        vm = normed_vector(fields, columns[4 * layer + 3])
         mix = jnp.dot(w_mix[layer], vm, preferred_element_type=f32)
         receive(base + 5, got_y.at[layer], y_rows[2])
         field = got_y[layer, :, 3 * own : 4 * own, :].reshape(chans, tok).astype(f32)
         out_s = (qs * field + mixed).astype(bf16)
         now_s = state_s[...] + jnp.dot(w_out_s[layer], out_s, preferred_element_type=f32)
-        sm = normed_scalar(now_s, column(gains[layer, 2:3, :]))
-        hidden = jax.nn.gelu(jnp.dot(w_up[layer], sm, preferred_element_type=f32)).astype(bf16)
+        sm = normed_scalar(now_s, columns[4 * layer + 2])
         gate = jax.nn.sigmoid(jnp.dot(w_gate[layer], sm, preferred_element_type=f32))
-        now_s = now_s + jnp.dot(w_down[layer], hidden, preferred_element_type=f32)
         now_v = [fields[j] + mix[:, j * tok : (j + 1) * tok] * gate for j in range(3)]
+        ready_s[...] = sm
+        state_s[...] = now_s
         if layer + 1 < depth:
-            state_s[...] = now_s
             for j in range(3):
                 state_v[j] = now_v[j]
         else:
-            scalars_out[...] = now_s.astype(bf16)
             for j in range(3):
                 vectors_out[j] = now_v[j].astype(bf16)
+            scalars_out[...] = finish_scalar(layer).astype(bf16)
     for layer in range(depth):
         for i in range(3):
             sent(6 * layer + i, sent_x.at[layer], x_rows[i])
             sent(6 * layer + 3 + i, sent_y.at[layer], y_rows[i])
+
+
+def place_results(scalars, vectors, scalars_out, vectors_out, sem):
+    copies = [
+        pltpu.make_async_copy(vectors, vectors_out, sem.at[0]),
+        pltpu.make_async_copy(scalars, scalars_out, sem.at[1]),
+    ]
+    for copy in copies:
+        copy.start()
+    for copy in copies:
+        copy.wait()
 
 
 def per_device(*arrays):
@@ -583,7 +604,7 @@
     arrays.append(local_tables(shards, tok))
     count = len(arrays)
     whole = pl.BlockSpec(memory_space=pltpu.VMEM)
-    return pl.pallas_call(
+    made = pl.pallas_call(
         functools.partial(layers_kernel, shards, count),
         out_shape=(
             jax.ShapeDtypeStruct(scalars.shape, bf16),
@@ -596,6 +617,8 @@
             pltpu.SemaphoreType.DMA((count,)),
             pltpu.VMEM((chans, tok), f32),
             pltpu.VMEM((3, chans, tok), f32),
+            pltpu.VMEM((4 * depth, chans, tok), f32),
+            pltpu.VMEM((chans, tok), bf16),
             pltpu.VMEM((chans, tok), bf16),
             pltpu.VMEM((chans, 3 * tok), bf16),
             pltpu.VMEM((half, 2 * tok, 2 * tok), bf16),
@@ -615,6 +638,16 @@
         ),
         name="hyena_layers",
     )(*arrays)
+    held = pl.BlockSpec(memory_space=pltpu.HBM)
+    return pl.pallas_call(
+        place_results,
+        out_shape=tuple(jax.ShapeDtypeStruct(one.shape, one.dtype) for one in made),
+        in_specs=[held, held],
+        out_specs=(held, held),
+        scratch_shapes=[pltpu.SemaphoreType.DMA((2,))],
+        compiler_params=pltpu.CompilerParams(vmem_limit_bytes=63 * 1024 * 1024),
+        name="place_results",
+    )(*made)
 
 
 def solution(mesh):

time: 51.4 us -> 57.1 us (1.11)
  Pallas kernels: 47.5 us -> 56.3 us
  local copies, waits for them, and re-layouts: 3.09 us -> 0 us
    pallas_call x0 -> x1, Pallas kernels: none -> 9.06 us  [per_device(): pl.pallas_call(place_results, out_shape=tuple((jax.ShapeDtypeStruct(one.s...]
    unnamed x2 -> x0, local copies, waits for them, and re-layouts: 3.09 us -> none
where the time goes in v3:
time: 57.1 us; the launch traced here: 57 us
  Pallas kernels  56.3 us (99%)
  between operations  0.64 us (1%)
    pallas_call x1, Pallas kernels, per_device(): pl.pallas_call(functools.partial(layers_kernel, shards, count), out_shape...  47.3 us
    pallas_call x1, Pallas kernels, per_device(): pl.pallas_call(place_results, out_shape=tuple((jax.ShapeDtypeStruct(one.s...  9.06 us

profile of v3, /device:TPU:0, one launch (start us, length us, event | category | flops | bytes accessed | tf_op | source)
XLA Modules:
  0.0 57.0 jit_solution(5983757391896656129)
XLA Ops:
  0.6 47.3 %hyena_layers.1 = (bf16[256,128]{1,0:T(8,128)(2,1)}, bf16[3,256,128]{2,1,0:T(8,128)(2,1)}) custom-call(bf16[256,128]{1,0:T(8,128)(2,1)} %refs_0_.1, bf16[3,256,128]{2,1,0:T(8,128)(2,1)} %refs_1_.1, bf16[2,768,256]{2,1,0:T(8,128)(2,1)} %refs_2_.1, bf16[2,768,256]{2,1,0:T(8,128)(2,1)} %refs_3_.1, bf16[2,256,256]{2,1,0:T(8,128)(2,1)} %refs_4_.1, ...), custom_call_target="tpu_custom_call" | custom-call | tf_op jit(solution)/shard_map/hyena_layers/pallas_call | solution.py:607
  47.9 9.1 %place_results.1 = (bf16[256,128]{1,0:T(8,128)(2,1)}, bf16[3,256,128]{2,1,0:T(8,128)(2,1)}) custom-call(bf16[256,128]{1,0:T(8,128)(2,1)} %get-tuple-element.4.scalars, bf16[3,256,128]{2,1,0:T(8,128)(2,1)} %get-tuple-element.5.vectors), custom_call_target="tpu_custom_call" | custom-call | tf_op jit(solution)/shard_map/place_results/pallas_call | solution.py:642

commit v4 on v3

--- a/solution.py
+++ b/solution.py
@@ -577,15 +577,9 @@
             sent(6 * layer + 3 + i, sent_y.at[layer], y_rows[i])
 
 
-def place_results(scalars, vectors, scalars_out, vectors_out, sem):
-    copies = [
-        pltpu.make_async_copy(vectors, vectors_out, sem.at[0]),
-        pltpu.make_async_copy(scalars, scalars_out, sem.at[1]),
-    ]
-    for copy in copies:
-        copy.start()
-    for copy in copies:
-        copy.wait()
+def place_results(scalars, vectors, scalars_out, vectors_out):
+    vectors_out[...] = vectors[...]
+    scalars_out[...] = scalars[...]
 
 
 def per_device(*arrays):
@@ -638,13 +632,11 @@
         ),
         name="hyena_layers",
     )(*arrays)
-    held = pl.BlockSpec(memory_space=pltpu.HBM)
     return pl.pallas_call(
         place_results,
         out_shape=tuple(jax.ShapeDtypeStruct(one.shape, one.dtype) for one in made),
-        in_specs=[held, held],
-        out_specs=(held, held),
-        scratch_shapes=[pltpu.SemaphoreType.DMA((2,))],
+        in_specs=[whole, whole],
+        out_specs=(whole, whole),
         compiler_params=pltpu.CompilerParams(vmem_limit_bytes=63 * 1024 * 1024),
         name="place_results",
     )(*made)

time: 57.1 us -> 49.7 us (0.87)
  Pallas kernels: 56.3 us -> 48.9 us
    pallas_call x1, Pallas kernels: 9.06 us -> 1.67 us  [per_device(): pl.pallas_call(place_results, out_shape=tuple((jax.ShapeDtypeStruct(one.s...]
where the time goes in v4:
time: 49.7 us; the launch traced here: 49.6 us
  Pallas kernels  48.9 us (98%)
  between operations  0.64 us (1%)
    pallas_call x1, Pallas kernels, per_device(): pl.pallas_call(functools.partial(layers_kernel, shards, count), out_shape...  47.3 us
    pallas_call x1, Pallas kernels, per_device(): pl.pallas_call(place_results, out_shape=tuple((jax.ShapeDtypeStruct(one.s...  1.67 us

profile of v4, /device:TPU:0, one launch (start us, length us, event | category | flops | bytes accessed | tf_op | source)
XLA Modules:
  0.0 49.6 jit_solution(894687445965487008)
XLA Ops:
  0.6 47.3 %hyena_layers.1 = (bf16[256,128]{1,0:T(8,128)(2,1)}, bf16[3,256,128]{2,1,0:T(8,128)(2,1)}) custom-call(bf16[256,128]{1,0:T(8,128)(2,1)} %refs_0_.1, bf16[3,256,128]{2,1,0:T(8,128)(2,1)} %refs_1_.1, bf16[2,768,256]{2,1,0:T(8,128)(2,1)} %refs_2_.1, bf16[2,768,256]{2,1,0:T(8,128)(2,1)} %refs_3_.1, bf16[2,256,256]{2,1,0:T(8,128)(2,1)} %refs_4_.1, ...), custom_call_target="tpu_custom_call" | custom-call | tf_op jit(solution)/shard_map/hyena_layers/pallas_call | solution.py:601
  47.9 1.7 %place_results.1 = (bf16[256,128]{1,0:T(8,128)(2,1)}, bf16[3,256,128]{2,1,0:T(8,128)(2,1)}) custom-call(bf16[256,128]{1,0:T(8,128)(2,1)} %get-tuple-element.4.scalars, bf16[3,256,128]{2,1,0:T(8,128)(2,1)} %get-tuple-element.5.vectors), custom_call_target="tpu_custom_call" | custom-call | tf_op jit(solution)/shard_map/place_results/pallas_call | solution.py:635
